TPU v7x, 32 devices: a whole 2x2x4 slice. The times are simulated.
32 devices in a mesh: replica: 2 (over x), segment: 4 (over z), tensor: 4 (over y, core).
Axes of the slice: x: 2, y: 2, z: 4, core: 2. Of those that a mesh axis runs over, the one named last changes fastest.
Arguments:
- x_in: bfloat16 [256, 8192], P('replica', 'tensor'), parts along dimension 0, may hold values from -6 to 6
- norm_gain: float32 [4, 8192], P('segment'), may hold values from 0.5 to 1.5
- in_index: int32 [4, 224, 72], P('segment', 'tensor'), may hold values from -1 to 127, as said below
- gate_blocks: bfloat16 [4, 224, 72, 4096], P('segment', 'tensor'), may hold values from -0.09375 to 0.09375
- up_blocks: bfloat16 [4, 224, 72, 4096], P('segment', 'tensor'), may hold values from -0.09375 to 0.09375
- out_index: int32 [4, 128, 126], P('segment', 'tensor'), may hold values from -1 to 223, as said below
- down_blocks: bfloat16 [4, 128, 126, 4096], P('segment', 'tensor'), may hold values from -0.0625 to 0.0625
Outputs:
- sections: bfloat16 [4, 256, 8192], P('segment', 'replica', 'tensor'), parts along dimension 1
There are 2 independent parts, one for each index of `replica`. A program takes and returns all parts, laid end to end along the dimension named above; an argument that names none is the same for every part. Nothing has to cross between parts.
Inputs may be any that keep to these rules, and one draw needn't show every extreme that they name: `in_index`: for each section and column block the entries name distinct row blocks, the kept ones first and -1 in the remaining slots; between 3 * 128 / 8 (rounded down) and 72 slots are kept, and in every section some column block keeps exactly 72 and another exactly the least. `out_index`: for each section and column block the entries name distinct row blocks, the kept ones first and -1 in the remaining slots; between 3 * 224 / 8 (rounded down) and 126 slots are kept, and in every section some column block keeps exactly 126 and another exactly the least.
All inputs are finite; a program needn't handle non-finite values.
Results may differ from a plain program's by a relative error of at most 0.0095.
Values may be sent and summed in bfloat16 or wider, within the bound.
A program may use at most 512 MiB of HBM per device.

v0:
```python
import jax
import jax.numpy as jnp
from jax import lax
from jax.sharding import PartitionSpec as P

D = 8192
FFW = 14336
BS = 64


def shifted(value, axis, by):
    length = lax.axis_size(axis)
    pairs = [(i, i + by) for i in range(length) if 0 <= i + by < length]
    return lax.ppermute(value, axis, pairs)


def densify(index, blocks, row_blocks):
    tile_count = index.shape[0]
    picks = (index[:, None, :] == jnp.arange(row_blocks, dtype=jnp.int32)[None, :, None]).astype(
        jnp.bfloat16
    )
    dense = jnp.einsum("crm,cmq->crq", picks, blocks, preferred_element_type=jnp.bfloat16)
    dense = dense.reshape(tile_count, row_blocks, BS, BS)
    return jnp.transpose(dense, (1, 2, 0, 3)).reshape(row_blocks * BS, tile_count * BS)


def local(x_in, norm_gain, in_index, gate_blocks, up_blocks, out_index, down_blocks):
    segment_count = lax.axis_size("segment")
    segment_at = lax.axis_index("segment")
    tokens, local_cols = x_in.shape
    gain_row = norm_gain[0]
    index_in = in_index[0]
    index_out = out_index[0]
    gate_dense = densify(index_in, gate_blocks[0], D // BS)
    up_dense = densify(index_in, up_blocks[0], D // BS)
    down_dense = densify(index_out, down_blocks[0], FFW // BS)
    rows_micro = tokens // 2
    group_count = tokens // rows_micro
    tick_count = group_count + segment_count - 1
    result = jnp.zeros((tokens, local_cols), jnp.bfloat16)
    carried = jnp.zeros((rows_micro, local_cols), jnp.bfloat16)
    for tick_now in range(tick_count):
        first_group = min(tick_now, group_count - 1)
        first_rows = x_in[first_group * rows_micro : (first_group + 1) * rows_micro]
        incoming = jnp.where(segment_at == 0, first_rows, carried)
        whole = lax.all_gather(incoming, "tensor", axis=1, tiled=True)
        wide = whole.astype(jnp.float32)
        stat = jnp.mean(wide * wide, axis=1, keepdims=True)
        section_normed = (wide * lax.rsqrt(stat + 1e-05) * gain_row[None, :]).astype(jnp.bfloat16)
        gate = jnp.dot(section_normed, gate_dense, preferred_element_type=jnp.float32)
        up_part = jnp.dot(section_normed, up_dense, preferred_element_type=jnp.float32)
        section_hidden = (jax.nn.silu(gate) * up_part).astype(jnp.bfloat16)
        mixed = jnp.dot(
            lax.all_gather(section_hidden, "tensor", axis=1, tiled=True),
            down_dense,
            preferred_element_type=jnp.float32,
        )
        produced = (incoming.astype(jnp.float32) + mixed).astype(jnp.bfloat16)
        micro_id = tick_now - segment_at
        is_valid = jnp.logical_and(micro_id >= 0, micro_id < group_count)
        offset = jnp.clip(micro_id, 0, group_count - 1) * rows_micro
        previous = lax.dynamic_slice_in_dim(result, offset, rows_micro, 0)
        result = lax.dynamic_update_slice_in_dim(
            result, jnp.where(is_valid, produced, previous), offset, 0
        )
        if tick_now + 1 < tick_count:
            carried = shifted(produced, "segment", 1)
    return result[None]


def solution(mesh):
    placed = (
        P("replica", "tensor"),
        P("segment", None),
        P("segment", "tensor", None),
        P("segment", "tensor", None, None),
        P("segment", "tensor", None, None),
        P("segment", "tensor", None),
        P("segment", "tensor", None, None),
    )
    return jax.shard_map(
        local,
        mesh=mesh,
        in_specs=placed,
        out_specs=P("segment", "replica", "tensor"),
        check_vma=False,
    )
```

profile of v0, /device:TPU:0, one launch (start us, length us, event | category | flops | bytes accessed | tf_op | source)
XLA Modules:
  0.0 1571.4 jit_solution(12304389915639571226)
XLA Ops:
  8.3 35.2 %fusion.4 = bf16[56,128,4096]{1,2,0:T(8,128)(2,1)} fusion(bf16[1,56,72,4096]{3,2,1,0:T(8,128)(2,1)} %param.10, s32[56,72]{1,0:T(8,128)} %bitcast.65), kind=kOutput, calls=%fused_computation.4 | convolution fusion | flops 4228374528 | bytes 91766528 | tf_op jit(solution)/shard_map/crm,cmq->crq/dot_general | solution.py:22
  43.5 34.5 %fusion.2 = bf16[56,128,4096]{1,2,0:T(8,128)(2,1)} fusion(bf16[1,56,72,4096]{3,2,1,0:T(8,128)(2,1)} %param.11, s32[56,72]{1,0:T(8,128)S(1)} %bitcast.66), kind=kOutput, calls=%fused_computation.2 | convolution fusion | flops 4228374528 | bytes 91766528 | tf_op jit(solution)/shard_map/crm,cmq->crq/dot_general | solution.py:22
  78.0 156.3 %copy.10 = bf16[128,64,56,64]{3,2,1,0:T(8,128)(2,1)} copy(bf16[128,64,56,64]{0,3,1,2:T(8,128)(2,1)} %bitcast.52) | data formatting | bytes 117440512 | tf_op jit(solution)/shard_map/transpose | solution.py:24
  234.2 140.7 %reshape.63 = bf16[8192,3584]{1,0:T(8,128)(2,1)} reshape(bf16[128,64,56,64]{3,2,1,0:T(8,128)(2,1)} %copy.10) | data formatting | bytes 117440512 | tf_op jit(solution)/shard_map/reshape | solution.py:24
  374.9 156.3 %copy.12 = bf16[128,64,56,64]{3,2,1,0:T(8,128)(2,1)} copy(bf16[128,64,56,64]{0,3,1,2:T(8,128)(2,1)} %bitcast.51) | data formatting | bytes 117440512 | tf_op jit(solution)/shard_map/transpose | solution.py:24
  531.2 140.7 %reshape.65 = bf16[8192,3584]{1,0:T(8,128)(2,1)} reshape(bf16[128,64,56,64]{3,2,1,0:T(8,128)(2,1)} %copy.12) | data formatting | bytes 117440512 | tf_op jit(solution)/shard_map/reshape | solution.py:24
  673.5 24.8 %fusion.43 = f32[64,3584]{1,0:T(8,128)S(1)} fusion(bf16[8192,3584]{1,0:T(8,128)(2,1)} %reshape.63, bf16[64,8192]{1,0:T(8,128)(2,1)} %all-gather.11.cloned.1.call-done, f32[8192]{0:T(1024)S(1)} %bitcast.55, f32[64]{0:T(128)S(1)} %add_rsqrt_fusion.4), kind=kOutput, calls=%fused_computation.56 | convolution fusion | flops 3760193536 | bytes 60719360 | tf_op jit(solution)/shard_map/dot_general | solution.py:50
  698.4 21.7 %fusion.6 = bf16[64,3584]{1,0:T(8,128)(2,1)} fusion(bf16[8192,3584]{1,0:T(8,128)(2,1)} %reshape.65, f32[64,3584]{1,0:T(8,128)S(1)} %fusion.43, bf16[64,8192]{1,0:T(8,128)(2,1)S(1)} %copy-done, f32[8192]{0:T(1024)S(1)} %bitcast.56, f32[64]{0:T(128)S(1)} %add_rsqrt_fusion.4), kind=kOutput, calls=%fused_computation.11 | convolution fusion | flops 3761569792 | bytes 61178112 | tf_op jit(solution)/shard_map/dot_general | solution.py:51
  720.2 45.9 %fusion = bf16[32,224,4096]{1,2,0:T(8,128)(2,1)} fusion(bf16[32,126,4096]{2,0,1:T(8,128)(2,1)} %bitcast.53, s32[32,126]{1,0:T(8,128)S(1)} %bitcast.67), kind=kOutput, calls=%fused_computation | convolution fusion | flops 7399655424 | bytes 91766528 | tf_op jit(solution)/shard_map/crm,cmq->crq/dot_general | solution.py:22
  766.1 139.2 %copy.15 = bf16[224,64,32,64]{3,2,1,0:T(8,128)(2,1)} copy(bf16[224,64,32,64]{0,3,1,2:T(8,128)(2,1)} %bitcast.11) | data formatting | bytes 117440512 | tf_op jit(solution)/shard_map/transpose | solution.py:24
  905.3 157.3 %reshape.67 = bf16[14336,2048]{1,0:T(8,128)(2,1)} reshape(bf16[224,64,32,64]{3,2,1,0:T(8,128)(2,1)} %copy.15) | data formatting | bytes 117440512 | tf_op jit(solution)/shard_map/reshape | solution.py:24
  1062.6 22.2 %select_dynamic-update-slice_fusion.3 = (bf16[128,2048]{1,0:T(8,128)(2,1)S(1)}, bf16[64,2048]{1,0:T(8,128)(2,1)S(1)}) fusion(bf16[128,2048]{1,0:T(8,128)(2,1)S(1)} %broadcast_in_dim.6, s32[]{:T(128)S(6)} %select_n.77, pred[]{:T(512)S(6)} %and.16, bf16[64,14336]{1,0:T(8,128)(2,1)} %all-gather.13.cloned.1.call-done, bf16[14336,2048]{1,0:T(8,128)(2,1)} %reshape.67, ...), kind=kOutput, calls=%fused_computation.63 | convolution fusion | flops 3758620672 | bytes 61341700 | tf_op jit(solution)/shard_map/dot_general | solution.py:53
  1096.2 18.9 %all-gather.15.cloned.1.call-done = bf16[64,8192]{1,0:T(8,128)(2,1)} async-done(((bf16[64,2048]{1,0:T(8,128)(2,1)}), bf16[64,8192]{1,0:T(8,128)(2,1)}) %all-gather.15.cloned.1.call-update) | async-done | bytes 1048592 | tf_op jit(solution)/shard_map/all_gather | solution.py:46
  1116.7 29.6 %fusion.40 = f32[64,3584]{1,0:T(8,128)S(1)} fusion(bf16[8192,3584]{1,0:T(8,128)(2,1)} %reshape.63, bf16[64,8192]{1,0:T(8,128)(2,1)} %all-gather.15.cloned.1.call-done, f32[64]{0:T(128)S(1)} %add_rsqrt_fusion.3, f32[8192]{0:T(1024)S(1)} %bitcast.57), kind=kOutput, calls=%fused_computation.55 | convolution fusion | flops 3760193536 | bytes 60719360 | tf_op jit(solution)/shard_map/dot_general | solution.py:50
  1146.3 21.8 %fusion.7 = bf16[64,3584]{1,0:T(8,128)(2,1)} fusion(bf16[8192,3584]{1,0:T(8,128)(2,1)} %reshape.65, f32[64,3584]{1,0:T(8,128)S(1)} %fusion.40, bf16[64,8192]{1,0:T(8,128)(2,1)S(1)} %copy-done.2, f32[64]{0:T(128)S(1)} %add_rsqrt_fusion.3, f32[8192]{0:T(1024)S(1)} %bitcast.58), kind=kOutput, calls=%fused_computation.12 | convolution fusion | flops 3761569792 | bytes 61178112 | tf_op jit(solution)/shard_map/dot_general | solution.py:51
  1168.1 21.2 %all-gather.17.cloned.1.call-done = bf16[64,14336]{1,0:T(8,128)(2,1)} async-done(((bf16[64,3584]{1,0:T(8,128)(2,1)}), bf16[64,14336]{1,0:T(8,128)(2,1)}) %all-gather.17.cloned.1.call-update) | async-done | bytes 1835024 | tf_op jit(solution)/shard_map/all_gather | solution.py:54
  1189.4 22.2 %select_dynamic-update-slice_fusion.2 = (bf16[128,2048]{1,0:T(8,128)(2,1)S(1)}, bf16[64,2048]{1,0:T(8,128)(2,1)S(1)}) fusion(bf16[128,2048]{1,0:T(8,128)(2,1)S(1)} %get-tuple-element.11, s32[]{:T(128)S(6)} %select_n.80, pred[]{:T(512)S(6)} %and.17, bf16[64,2048]{1,0:T(8,128)(2,1)S(1)} %copy-done.10, bf16[64,14336]{1,0:T(8,128)(2,1)} %all-gather.17.cloned.1.call-done, ...), kind=kOutput, calls=%fused_computation.62 | convolution fusion | flops 3758620672 | bytes 61603844 | tf_op jit(solution)/shard_map/dot_general | solution.py:53
  1221.7 17.8 %all-gather.19.cloned.1.call-done = bf16[64,8192]{1,0:T(8,128)(2,1)} async-done(((bf16[64,2048]{1,0:T(8,128)(2,1)}), bf16[64,8192]{1,0:T(8,128)(2,1)}) %all-gather.19.cloned.1.call-update) | async-done | bytes 1048592 | tf_op jit(solution)/shard_map/all_gather | solution.py:46
  1241.1 21.1 %fusion.37 = f32[64,3584]{1,0:T(8,128)S(1)} fusion(bf16[8192,3584]{1,0:T(8,128)(2,1)} %reshape.63, bf16[64,8192]{1,0:T(8,128)(2,1)} %all-gather.19.cloned.1.call-done, f32[64]{0:T(128)S(1)} %add_rsqrt_fusion.2, f32[8192]{0:T(1024)S(1)} %bitcast.59), kind=kOutput, calls=%fused_computation.54 | convolution fusion | flops 3760193536 | bytes 60719360 | tf_op jit(solution)/shard_map/dot_general | solution.py:50
  1262.2 21.8 %fusion.8 = bf16[64,3584]{1,0:T(8,128)(2,1)} fusion(bf16[8192,3584]{1,0:T(8,128)(2,1)} %reshape.65, f32[64,3584]{1,0:T(8,128)S(1)} %fusion.37, bf16[64,8192]{1,0:T(8,128)(2,1)S(1)} %copy-done.3, f32[64]{0:T(128)S(1)} %add_rsqrt_fusion.2, f32[8192]{0:T(1024)S(1)} %bitcast.60), kind=kOutput, calls=%fused_computation.13 | convolution fusion | flops 3761569792 | bytes 61178112 | tf_op jit(solution)/shard_map/dot_general | solution.py:51
  1284.0 21.2 %all-gather.21.cloned.1.call-done = bf16[64,14336]{1,0:T(8,128)(2,1)} async-done(((bf16[64,3584]{1,0:T(8,128)(2,1)}), bf16[64,14336]{1,0:T(8,128)(2,1)}) %all-gather.21.cloned.1.call-update) | async-done | bytes 1835024 | tf_op jit(solution)/shard_map/all_gather | solution.py:54
  1305.3 22.4 %select_dynamic-update-slice_fusion.1 = (bf16[128,2048]{1,0:T(8,128)(2,1)S(1)}, bf16[64,2048]{1,0:T(8,128)(2,1)S(1)}) fusion(bf16[128,2048]{1,0:T(8,128)(2,1)S(1)} %get-tuple-element.9, s32[]{:T(128)S(6)} %select_n.84, pred[]{:T(512)S(6)} %and.18, bf16[64,2048]{1,0:T(8,128)(2,1)S(1)} %copy-done.11, bf16[64,14336]{1,0:T(8,128)(2,1)} %all-gather.21.cloned.1.call-done, ...), kind=kOutput, calls=%fused_computation.61 | convolution fusion | flops 3758620672 | bytes 61603844 | tf_op jit(solution)/shard_map/dot_general | solution.py:53
  1337.8 17.8 %all-gather.23.cloned.1.call-done = bf16[64,8192]{1,0:T(8,128)(2,1)} async-done(((bf16[64,2048]{1,0:T(8,128)(2,1)}), bf16[64,8192]{1,0:T(8,128)(2,1)}) %all-gather.23.cloned.1.call-update) | async-done | bytes 1048592 | tf_op jit(solution)/shard_map/all_gather | solution.py:46
  1357.2 21.1 %fusion.34 = f32[64,3584]{1,0:T(8,128)S(1)} fusion(bf16[8192,3584]{1,0:T(8,128)(2,1)} %reshape.63, bf16[64,8192]{1,0:T(8,128)(2,1)} %all-gather.23.cloned.1.call-done, f32[64]{0:T(128)S(1)} %add_rsqrt_fusion.1, f32[8192]{0:T(1024)S(1)} %bitcast.61), kind=kOutput, calls=%fused_computation.53 | convolution fusion | flops 3760193536 | bytes 60719360 | tf_op jit(solution)/shard_map/dot_general | solution.py:50
  1378.3 21.8 %fusion.9 = bf16[64,3584]{1,0:T(8,128)(2,1)} fusion(bf16[8192,3584]{1,0:T(8,128)(2,1)} %reshape.65, f32[64,3584]{1,0:T(8,128)S(1)} %fusion.34, bf16[64,8192]{1,0:T(8,128)(2,1)S(1)} %copy-done.4, f32[64]{0:T(128)S(1)} %add_rsqrt_fusion.1, f32[8192]{0:T(1024)S(1)} %bitcast.62), kind=kOutput, calls=%fused_computation.14 | convolution fusion | flops 3761569792 | bytes 61178112 | tf_op jit(solution)/shard_map/dot_general | solution.py:51
  1400.1 21.2 %all-gather.25.cloned.1.call-done = bf16[64,14336]{1,0:T(8,128)(2,1)} async-done(((bf16[64,3584]{1,0:T(8,128)(2,1)}), bf16[64,14336]{1,0:T(8,128)(2,1)}) %all-gather.25.cloned.1.call-update) | async-done | bytes 1835024 | tf_op jit(solution)/shard_map/all_gather | solution.py:54
  1421.3 22.2 %select_dynamic-update-slice_fusion = (bf16[128,2048]{1,0:T(8,128)(2,1)S(1)}, bf16[64,2048]{1,0:T(8,128)(2,1)S(1)}) fusion(bf16[128,2048]{1,0:T(8,128)(2,1)S(1)} %get-tuple-element.7, s32[]{:T(128)S(6)} %select_n.88, pred[]{:T(512)S(6)} %and.19, bf16[64,2048]{1,0:T(8,128)(2,1)S(1)} %copy-done.9, bf16[64,14336]{1,0:T(8,128)(2,1)} %all-gather.25.cloned.1.call-done, ...), kind=kOutput, calls=%fused_computation.60 | convolution fusion | flops 3758620672 | bytes 61603844 | tf_op jit(solution)/shard_map/dot_general | solution.py:53
  1453.7 17.8 %all-gather.27.cloned.1.call-done = bf16[64,8192]{1,0:T(8,128)(2,1)} async-done(((bf16[64,2048]{1,0:T(8,128)(2,1)}), bf16[64,8192]{1,0:T(8,128)(2,1)}) %all-gather.27.cloned.1.call-update) | async-done | bytes 1048592 | tf_op jit(solution)/shard_map/all_gather | solution.py:46
  1473.1 25.0 %fusion.31 = f32[64,3584]{1,0:T(8,128)S(1)} fusion(bf16[8192,3584]{1,0:T(8,128)(2,1)} %reshape.63, bf16[64,8192]{1,0:T(8,128)(2,1)} %all-gather.27.cloned.1.call-done, f32[64]{0:T(128)S(1)} %add_rsqrt_fusion, f32[8192]{0:T(1024)S(1)} %bitcast.63), kind=kOutput, calls=%fused_computation.52 | convolution fusion | flops 3760193536 | bytes 60719360 | tf_op jit(solution)/shard_map/dot_general | solution.py:50
  1498.1 21.8 %fusion.10 = bf16[64,3584]{1,0:T(8,128)(2,1)} fusion(bf16[8192,3584]{1,0:T(8,128)(2,1)} %reshape.65, f32[64,3584]{1,0:T(8,128)S(1)} %fusion.31, bf16[64,8192]{1,0:T(8,128)(2,1)S(1)} %copy-done.1, f32[64]{0:T(128)S(1)} %add_rsqrt_fusion, f32[8192]{0:T(1024)S(1)} %bitcast.64), kind=kOutput, calls=%fused_computation.15 | convolution fusion | flops 3761569792 | bytes 61178112 | tf_op jit(solution)/shard_map/dot_general | solution.py:51
  1520.7 20.5 %all-gather.29.cloned.1.call-done = bf16[64,14336]{1,0:T(8,128)(2,1)} async-done(((bf16[64,3584]{1,0:T(8,128)(2,1)}), bf16[64,14336]{1,0:T(8,128)(2,1)}) %all-gather.29.cloned.1.call-update) | async-done | bytes 1835024 | tf_op jit(solution)/shard_map/all_gather | solution.py:54
  1541.2 22.9 %fusion.47 = bf16[1,128,2048]{2,1,0:T(8,128)(2,1)} fusion(bf16[1,128,2048]{2,1,0:T(8,128)(2,1)} %copy.26, s32[]{:T(128)S(6)} %select_n.92, bf16[64,2048]{1,0:T(8,128)(2,1)S(1)} %copy-done.8, bf16[128,2048]{1,0:T(8,128)(2,1)S(1)} %get-tuple-element.5, pred[]{:T(512)S(6)} %and.20, bf16[64,14336]{1,0:T(8,128)(2,1)} %all-gather.29.cloned.1.call-done, ...), kind=kOutput, calls=%fused_computation.59 | convolution fusion | flops 3758620672 | bytes 61341700 | tf_op jit(solution)/shard_map/dot_general | solution.py:53
  (75 shorter events, 52.2 us)
Async XLA Ops:
  6.5 665.4 %all-gather.11.cloned.1.call-start = ((), (), s32[]{:S(2)}) async-start(), calls=%async_computation | async-start | bytes 1310720 | tf_op jit(solution)/shard_map/all_gather | solution.py:46
  8.2 1054.3 %all-gather.13.cloned.1.call-start = ((), (), s32[]{:S(2)}) async-start(), calls=%async_computation.1 | async-start | bytes 2293760 | tf_op jit(solution)/shard_map/all_gather | solution.py:54
  8.3 35.2 %copy-start.12 = (s32[1,56,72]{2,1,0:T(8,128)S(1)}, s32[1,56,72]{2,1,0:T(8,128)}, u32[]{:S(2)}) copy-start(s32[1,56,72]{2,1,0:T(8,128)} %param.9) | copy-start | bytes 48388
  531.2 142.3 %copy-start.5 = (f32[1,8192]{1,0:T(1,128)S(1)}, f32[1,8192]{1,0:T(1,128)}, u32[]{:S(2)}) copy-start(f32[1,8192]{1,0:T(1,128)} %param.8) | copy-start | bytes 98308
  673.5 24.9 %copy-start = (bf16[64,8192]{1,0:T(8,128)(2,1)S(1)}, bf16[64,8192]{1,0:T(8,128)(2,1)}, u32[]{:S(2)}) copy-start(bf16[64,8192]{1,0:T(8,128)(2,1)} %all-gather.11.cloned.1.call-done) | copy-start | bytes 3145732
  698.4 21.8 %copy-start.13 = (s32[1,32,126]{2,1,0:T(8,128)S(1)}, s32[1,32,126]{2,1,0:T(8,128)}, u32[]{:S(2)}) copy-start(s32[1,32,126]{2,1,0:T(8,128)} %param.12) | copy-start | bytes 48388
  720.1 395.0 %all-gather.15.cloned.1.call-start = ((), (), s32[]{:S(2)}) async-start(), calls=%async_computation.2 | async-start | bytes 1310720 | tf_op jit(solution)/shard_map/all_gather | solution.py:46
  905.3 157.3 %copy-start.7 = (bf16[64,2048]{1,0:T(8,128)(2,1)S(1)}, bf16[64,2048]{1,0:T(8,128)(2,1)}, u32[]{:S(2)}) copy-start(bf16[64,2048]{1,0:T(8,128)(2,1)} %slice_select_fusion) | copy-start | bytes 786436
  1062.6 32.8 %copy-start.6 = (bf16[128,2048]{1,0:T(8,128)(2,1)S(1)}, bf16[128,2048]{1,0:T(8,128)(2,1)}, u32[]{:S(2)}) copy-start(bf16[128,2048]{1,0:T(8,128)(2,1)} %param.7) | copy-start | bytes 1572868
  1084.9 10.5 collective-permute-start
  1096.1 93.2 %all-gather.17.cloned.1.call-start = ((), (), s32[]{:S(2)}) async-start(), calls=%async_computation.3 | async-start | bytes 2293760 | tf_op jit(solution)/shard_map/all_gather | solution.py:54
  1116.6 29.6 %copy-start.2 = (bf16[64,8192]{1,0:T(8,128)(2,1)S(1)}, bf16[64,8192]{1,0:T(8,128)(2,1)}, u32[]{:S(2)}) copy-start(bf16[64,8192]{1,0:T(8,128)(2,1)} %all-gather.15.cloned.1.call-done) | copy-start | bytes 3145732
  1146.3 43.1 %copy-start.10 = (bf16[64,2048]{1,0:T(8,128)(2,1)S(1)}, bf16[64,2048]{1,0:T(8,128)(2,1)}, u32[]{:S(2)}) copy-start(bf16[64,2048]{1,0:T(8,128)(2,1)} %broadcast_select_fusion.3) | copy-start | bytes 786436
  1168.1 71.5 %all-gather.19.cloned.1.call-start = ((), (), s32[]{:S(2)}) async-start(), calls=%async_computation.4 | async-start | bytes 1310720 | tf_op jit(solution)/shard_map/all_gather | solution.py:46
  1211.6 9.3 collective-permute-start.1
  1221.7 83.6 %all-gather.21.cloned.1.call-start = ((), (), s32[]{:S(2)}) async-start(), calls=%async_computation.5 | async-start | bytes 2293760 | tf_op jit(solution)/shard_map/all_gather | solution.py:54
  1241.1 21.1 %copy-start.3 = (bf16[64,8192]{1,0:T(8,128)(2,1)S(1)}, bf16[64,8192]{1,0:T(8,128)(2,1)}, u32[]{:S(2)}) copy-start(bf16[64,8192]{1,0:T(8,128)(2,1)} %all-gather.19.cloned.1.call-done) | copy-start | bytes 3145732
  1262.2 43.1 %copy-start.11 = (bf16[64,2048]{1,0:T(8,128)(2,1)S(1)}, bf16[64,2048]{1,0:T(8,128)(2,1)}, u32[]{:S(2)}) copy-start(bf16[64,2048]{1,0:T(8,128)(2,1)} %broadcast_select_fusion.2) | copy-start | bytes 786436
  1284.0 71.7 %all-gather.23.cloned.1.call-start = ((), (), s32[]{:S(2)}) async-start(), calls=%async_computation.6 | async-start | bytes 1310720 | tf_op jit(solution)/shard_map/all_gather | solution.py:46
  1327.7 9.3 collective-permute-start.2
  1337.8 83.6 %all-gather.25.cloned.1.call-start = ((), (), s32[]{:S(2)}) async-start(), calls=%async_computation.7 | async-start | bytes 2293760 | tf_op jit(solution)/shard_map/all_gather | solution.py:54
  1357.2 21.1 %copy-start.4 = (bf16[64,8192]{1,0:T(8,128)(2,1)S(1)}, bf16[64,8192]{1,0:T(8,128)(2,1)}, u32[]{:S(2)}) copy-start(bf16[64,8192]{1,0:T(8,128)(2,1)} %all-gather.23.cloned.1.call-done) | copy-start | bytes 3145732
  1378.3 43.1 %copy-start.9 = (bf16[64,2048]{1,0:T(8,128)(2,1)S(1)}, bf16[64,2048]{1,0:T(8,128)(2,1)}, u32[]{:S(2)}) copy-start(bf16[64,2048]{1,0:T(8,128)(2,1)} %broadcast_select_fusion.1) | copy-start | bytes 786436
  1400.1 71.5 %all-gather.27.cloned.1.call-start = ((), (), s32[]{:S(2)}) async-start(), calls=%async_computation.8 | async-start | bytes 1310720 | tf_op jit(solution)/shard_map/all_gather | solution.py:46
  1443.5 9.3 collective-permute-start.3
  1453.7 87.5 %all-gather.29.cloned.1.call-start = ((), (), s32[]{:S(2)}) async-start(), calls=%async_computation.9 | async-start | bytes 2293760 | tf_op jit(solution)/shard_map/all_gather | solution.py:54
  1473.1 25.0 %copy-start.1 = (bf16[64,8192]{1,0:T(8,128)(2,1)S(1)}, bf16[64,8192]{1,0:T(8,128)(2,1)}, u32[]{:S(2)}) copy-start(bf16[64,8192]{1,0:T(8,128)(2,1)} %all-gather.27.cloned.1.call-done) | copy-start | bytes 3145732
  1498.1 43.1 %copy-start.8 = (bf16[64,2048]{1,0:T(8,128)(2,1)S(1)}, bf16[64,2048]{1,0:T(8,128)(2,1)}, u32[]{:S(2)}) copy-start(bf16[64,2048]{1,0:T(8,128)(2,1)} %broadcast_select_fusion) | copy-start | bytes 786436
Sparse Core Ops, SparseCore 0:
  8.9 19.4 all-gather.10
  720.2 23.8 all-gather.12
  1096.2 18.8 all-gather.14
  1168.2 21.1 all-gather.16
  1221.8 17.7 all-gather.18
  1284.1 21.1 all-gather.20
  1337.9 17.7 all-gather.22
  1400.2 21.1 all-gather.24
  1453.8 17.7 all-gather.26
  1520.0 21.1 all-gather.28
where the time goes:
time: 1600 us; the launch traced here: 1570 us
  local copies, waits for them, and re-layouts  891 us (56%)
  matrix products  458 us (29%)
  waiting for transfers between devices  180 us (11%)
    transpose x3, local copies, waits for them, and re-layouts, densify(): jnp.transpose(dense, (1, 2, 0, 3)).reshape(row_blocks * BS, tile_count * BS)  452 us
    reshape x3, local copies, waits for them, and re-layouts, densify(): jnp.transpose(dense, (1, 2, 0, 3)).reshape(row_blocks * BS, tile_count * BS)  439 us
    dot_general x5, matrix products, local(): jnp.dot(section_normed, gate_dense, preferred_element_type=jnp.float32)  122 us
    dot_general x3, matrix products, densify(): jnp.einsum('crm,cmq->crq', picks, blocks, preferred_element_type=jnp.bflo...  116 us
    dot_general x5, matrix products, local(): jnp.dot(lax.all_gather(section_hidden, 'tensor', axis=1, tiled=True), dow...  112 us
    dot_general x5, matrix products, local(): jnp.dot(section_normed, up_dense, preferred_element_type=jnp.float32)  109 us
    all_gather x5, waiting for transfers between devices, local(): lax.all_gather(section_hidden, 'tensor', axis=1, tiled=True)  84.2 us
    all_gather x5, waiting for transfers between devices, local(): whole = lax.all_gather(incoming, 'tensor', axis=1, tiled=True)  72.4 us
  transfers between devices with their start and end apart: 14, of which 12 were waited for; matrix products, arithmetic and copies ran while one was open for 64% of the time, Pallas kernels for 0%

commit v1 on v0

v1 whole, which is shorter than its diff:
```python
import jax
import jax.numpy as jnp
from jax import lax
from jax.experimental import pallas as pl
from jax.experimental.pallas import tpu as pltpu
from jax.sharding import PartitionSpec as P

BS = 64
LANES = 2 * BS
VMEM_LIMIT = 56 * 1024 * 1024


def swap_halves(value):
    return jnp.concatenate([value[:, BS:], value[:, :BS]], axis=1)


def picks_of(index_row, row_blocks):
    slots = index_row.shape[1]
    rows = lax.broadcasted_iota(jnp.int32, (row_blocks, slots), 0)
    return (index_row == rows).astype(jnp.float32).astype(jnp.bfloat16)


def expand_in_kernel(row_blocks, index_ref, gate_ref, up_ref, out_ref):
    picks = picks_of(index_ref[0], row_blocks)
    slots = gate_ref.shape[1]
    low = lax.broadcasted_iota(jnp.int32, (slots, LANES), 1) < BS
    for pair in range(BS // 2):
        gate = gate_ref[0, :, pair * LANES : (pair + 1) * LANES]
        up = up_ref[0, :, pair * LANES : (pair + 1) * LANES]
        both = jnp.concatenate(
            [jnp.where(low, gate, swap_halves(up)), jnp.where(low, swap_halves(gate), up)], axis=1
        )
        dense = jnp.dot(picks, both, preferred_element_type=jnp.float32).astype(jnp.bfloat16)
        at = 2 * pair * row_blocks
        out_ref[at : at + row_blocks, :] = dense[:, :LANES]
        out_ref[at + row_blocks : at + 2 * row_blocks, :] = dense[:, LANES:]


def expand_in(index, gate_blocks, up_blocks, row_blocks):
    tiles, slots, size = gate_blocks.shape
    padded = tiles + tiles % 2
    return pl.pallas_call(
        lambda *refs: expand_in_kernel(row_blocks, *refs),
        grid=(tiles,),
        in_specs=[
            pl.BlockSpec((1, 1, slots), lambda c: (c, 0, 0)),
            pl.BlockSpec((1, slots, size), lambda c: (c, 0, 0)),
            pl.BlockSpec((1, slots, size), lambda c: (c, 0, 0)),
        ],
        out_specs=pl.BlockSpec((row_blocks * BS, LANES), lambda c: (0, c)),
        out_shape=jax.ShapeDtypeStruct((row_blocks * BS, padded * LANES), jnp.bfloat16),
        compiler_params=pltpu.CompilerParams(vmem_limit_bytes=VMEM_LIMIT),
        name="expand_in",
    )(index[:, None, :], gate_blocks, up_blocks)


def expand_out_kernel(row_blocks, index_ref, blocks_ref, out_ref):
    first = picks_of(index_ref[0, 0:1, :], row_blocks)
    second = picks_of(index_ref[0, 1:2, :], row_blocks)
    low = lax.broadcasted_iota(jnp.int32, (row_blocks, LANES), 1) < BS
    for quad in range(BS // 4):
        cols = slice(quad * 2 * LANES, (quad + 1) * 2 * LANES)
        left = jnp.dot(first, blocks_ref[0, :, cols], preferred_element_type=jnp.float32)
        right = jnp.dot(second, blocks_ref[1, :, cols], preferred_element_type=jnp.float32)
        for half in range(2):
            a = left[:, half * LANES : (half + 1) * LANES]
            b = right[:, half * LANES : (half + 1) * LANES]
            at = (4 * quad + 2 * half) * row_blocks
            out_ref[at : at + row_blocks, :] = jnp.where(low, a, pltpu.roll(b, BS, 1)).astype(jnp.bfloat16)
            out_ref[at + row_blocks : at + 2 * row_blocks, :] = jnp.where(
                low, pltpu.roll(a, BS, 1), b
            ).astype(jnp.bfloat16)


def expand_out(index, blocks, row_blocks):
    tiles, slots, size = blocks.shape
    return pl.pallas_call(
        lambda *refs: expand_out_kernel(row_blocks, *refs),
        grid=(tiles // 2,),
        in_specs=[
            pl.BlockSpec((1, 2, slots), lambda c: (c, 0, 0)),
            pl.BlockSpec((2, slots, size), lambda c: (c, 0, 0)),
        ],
        out_specs=pl.BlockSpec((row_blocks * BS, LANES), lambda c: (0, c)),
        out_shape=jax.ShapeDtypeStruct((row_blocks * BS, tiles * BS), jnp.bfloat16),
        compiler_params=pltpu.CompilerParams(vmem_limit_bytes=VMEM_LIMIT),
        name="expand_out",
    )(index.reshape(tiles // 2, 2, slots), blocks)


def gate_up_kernel(x_ref, w_ref, out_ref):
    both = jnp.dot(x_ref[...], w_ref[...], preferred_element_type=jnp.float32)
    a, b = both[:, :LANES], both[:, LANES:]
    low = lax.broadcasted_iota(jnp.int32, a.shape, 1) < BS
    gate = jnp.where(low, a, pltpu.roll(b, BS, 1))
    up = jnp.where(low, pltpu.roll(a, BS, 1), b)
    out_ref[...] = (gate / (1.0 + jnp.exp(-gate)) * up).astype(jnp.bfloat16)


def gate_up(x, weights):
    rows, depth = x.shape
    steps = weights.shape[1] // (2 * LANES)
    return pl.pallas_call(
        gate_up_kernel,
        grid=(steps,),
        in_specs=[
            pl.BlockSpec((rows, depth), lambda n: (0, 0)),
            pl.BlockSpec((depth, 2 * LANES), lambda n: (0, n)),
        ],
        out_specs=pl.BlockSpec((rows, LANES), lambda n: (0, n)),
        out_shape=jax.ShapeDtypeStruct((rows, steps * LANES), jnp.bfloat16),
        compiler_params=pltpu.CompilerParams(vmem_limit_bytes=VMEM_LIMIT),
        name="gate_up",
    )(x, weights)


def down_kernel(h_ref, w_ref, x_ref, out_ref):
    mixed = jnp.dot(h_ref[...], w_ref[...], preferred_element_type=jnp.float32)
    out_ref[...] = (x_ref[...].astype(jnp.float32) + mixed).astype(jnp.bfloat16)


def down(hidden, weights, x):
    rows, depth = hidden.shape
    cols = weights.shape[1]
    width = 2 * LANES if cols % (2 * LANES) == 0 else LANES
    return pl.pallas_call(
        down_kernel,
        grid=(cols // width,),
        in_specs=[
            pl.BlockSpec((rows, depth), lambda n: (0, 0)),
            pl.BlockSpec((depth, width), lambda n: (0, n)),
            pl.BlockSpec((rows, width), lambda n: (0, n)),
        ],
        out_specs=pl.BlockSpec((rows, width), lambda n: (0, n)),
        out_shape=jax.ShapeDtypeStruct((rows, cols), jnp.bfloat16),
        compiler_params=pltpu.CompilerParams(vmem_limit_bytes=VMEM_LIMIT),
        name="down",
    )(hidden, weights, x)


def by_inner_row(value):
    rows, cols = value.shape
    return value.reshape(rows, cols // BS, BS).swapaxes(1, 2).reshape(rows, cols)


def local(x_in, norm_gain, in_index, gate_blocks, up_blocks, out_index, down_blocks):
    segment_count = lax.axis_size("segment")
    tensor_count = lax.axis_size("tensor")
    segment_at = lax.axis_index("segment")
    gain_row = norm_gain[0]
    local_hidden = in_index.shape[1] * BS
    weights_in = expand_in(in_index[0], gate_blocks[0], up_blocks[0], gain_row.shape[0] // BS)
    weights_out = expand_out(out_index[0], down_blocks[0], tensor_count * local_hidden // BS)
    pairs = [(i, i + 1) for i in range(segment_count - 1)]
    incoming = x_in
    result = jnp.zeros_like(x_in)
    for tick in range(segment_count):
        whole = lax.all_gather(incoming, "tensor", axis=1, tiled=True)
        wide = whole.astype(jnp.float32)
        stat = jnp.mean(wide * wide, axis=1, keepdims=True)
        normed = (wide * lax.rsqrt(stat + 1e-05) * gain_row[None, :]).astype(jnp.bfloat16)
        hidden = gate_up(by_inner_row(normed), weights_in)[:, :local_hidden]
        hidden = lax.all_gather(hidden, "tensor", axis=1, tiled=True)
        produced = down(by_inner_row(hidden), weights_out, incoming)
        result = jnp.where(segment_at == tick, produced, result)
        if tick + 1 < segment_count:
            incoming = lax.ppermute(produced, "segment", pairs)
    return result[None]


def solution(mesh):
    placed = (
        P("replica", "tensor"),
        P("segment", None),
        P("segment", "tensor", None),
        P("segment", "tensor", None, None),
        P("segment", "tensor", None, None),
        P("segment", "tensor", None),
        P("segment", "tensor", None, None),
    )
    return jax.shard_map(
        local,
        mesh=mesh,
        in_specs=placed,
        out_specs=P("segment", "replica", "tensor"),
        check_vma=False,
    )
```

time: 1600 us -> 802 us (0.50); the launches traced: 1570 us -> 791 us
  local copies, waits for them, and re-layouts: 891 us -> 144 us
  matrix products: 458 us -> 0 us
  Pallas kernels: 0 us -> 400 us
  waiting for transfers between devices: 180 us -> 202 us
    dot_general x18 -> x0, matrix products: 458 us -> none  [the longest x5 122 us: local(): jnp.dot(section_normed, gate_dense, preferred_element_type=jnp.float32)]
    reshape x3 -> x4, local copies, waits for them, and re-layouts: 439 us -> 23.9 us  [by_inner_row(): value.reshape(rows, cols // BS, BS).swapaxes(1, 2).reshape(rows, cols)]
    transpose x3 -> x8, local copies, waits for them, and re-layouts: 452 us -> 40.2 us  [by_inner_row(): value.reshape(rows, cols // BS, BS).swapaxes(1, 2).reshape(rows, cols)]
    pallas_call x0 -> x10, Pallas kernels: none -> 400 us  [the longest x4 189 us: gate_up(): pl.pallas_call(gate_up_kernel, grid=(steps,), in_specs=[pl.BlockSpec((row...]
    unnamed x29 -> x19, local copies, waits for them, and re-layouts: 0.86 us -> 45.7 us
    all_gather x0 -> x4, local copies, waits for them, and re-layouts: none -> 24 us  [local(): hidden = lax.all_gather(hidden, 'tensor', axis=1, tiled=True)]
    ppermute x4 -> x3, waiting for transfers between devices: 23.3 us -> 35.1 us  [local(): incoming = lax.ppermute(produced, 'segment', pairs)]
    all_gather x5 -> x4, waiting for transfers between devices: 84.2 us -> 94.9 us  [local(): hidden = lax.all_gather(hidden, 'tensor', axis=1, tiled=True)]
  transfers between devices with their start and end apart: 14 -> 11, of which waited for: 12 -> 9; matrix products, arithmetic and copies ran while one was open for 64% -> 4% of each run, Pallas kernels for 0% -> 16%
where the time goes in v1:
time: 802 us; the launch traced here: 791 us
  Pallas kernels  400 us (50%)
  waiting for transfers between devices  202 us (25%)
  local copies, waits for them, and re-layouts  144 us (18%)
  other arithmetic  17.9 us (2%)
  between operations  13.9 us (2%)
  starting transfers between devices  13.3 us (2%)
    pallas_call x4, Pallas kernels, gate_up(): pl.pallas_call(gate_up_kernel, grid=(steps,), in_specs=[pl.BlockSpec((row...  189 us
    all_gather x4, waiting for transfers between devices, local(): hidden = lax.all_gather(hidden, 'tensor', axis=1, tiled=True)  94.9 us
    pallas_call x4, Pallas kernels, down(): pl.pallas_call(down_kernel, grid=(cols // width,), in_specs=[pl.BlockSpec...  86.7 us
    pallas_call x1, Pallas kernels, expand_in(): pl.pallas_call(lambda *refs: expand_in_kernel(row_blocks, *refs), grid=(t...  85.9 us
    all_gather x4, waiting for transfers between devices, local(): whole = lax.all_gather(incoming, 'tensor', axis=1, tiled=True)  71.3 us
    unnamed x19, local copies, waits for them, and re-layouts  45.7 us
    transpose x8, local copies, waits for them, and re-layouts, by_inner_row(): value.reshape(rows, cols // BS, BS).swapaxes(1, 2).reshape(rows, cols)  40.2 us
    pallas_call x1, Pallas kernels, expand_out(): pl.pallas_call(lambda *refs: expand_out_kernel(row_blocks, *refs), grid=(...  38.2 us
  transfers between devices with their start and end apart: 11, of which 9 were waited for; matrix products, arithmetic and copies ran while one was open for 4% of the time, Pallas kernels for 16%

profile of v1, /device:TPU:0, one launch (start us, length us, event | category | flops | bytes accessed | tf_op | source)
XLA Modules:
  0.0 791.2 jit_solution(5845310130178138569)
XLA Ops:
  7.3 85.9 %expand_in.1.w_ref = bf16[8192,7168]{1,0:T(8,128)(2,1)} custom-call(s32[56,1,72]{2,1,0:T(1,128)} %bitcast.81, bf16[56,72,4096]{2,1,0:T(8,128)(2,1)} %bitcast.55, bf16[56,72,4096]{2,1,0:T(8,128)(2,1)} %bitcast.56), custom_call_target="tpu_custom_call" | custom-call | tf_op jit(solution)/shard_map/expand_in/pallas_call | solution.py:42
  106.9 47.4 %gate_up.4 = bf16[128,3584]{1,0:T(8,128)(2,1)} custom-call(bf16[128,8192]{1,0:T(8,128)(2,1)} %bitcast.66, bf16[8192,7168]{1,0:T(8,128)(2,1)} %expand_in.1.w_ref), custom_call_target="tpu_custom_call" | custom-call | tf_op jit(solution)/shard_map/gate_up/pallas_call | solution.py:103
  154.9 30.6 %copy.47 = bf16[1,32,126,4096]{3,2,1,0:T(8,128)(2,1)} copy(bf16[1,32,126,4096]{3,1,2,0:T(8,128)(2,1)} %param.13) | data formatting | bytes 66060288 | tf_op args[6]
  185.5 38.2 %expand_out.1.w_ref = bf16[14336,2048]{1,0:T(8,128)(2,1)} custom-call(s32[16,2,126]{2,1,0:T(2,128)} %bitcast.82, bf16[32,126,4096]{2,1,0:T(8,128)(2,1)} %bitcast.54), custom_call_target="tpu_custom_call" | custom-call | tf_op jit(solution)/shard_map/expand_out/pallas_call | solution.py:77
  223.7 6.0 copy.19
  229.8 6.2 copy.20
  236.0 5.9 copy.22.h_ref
  241.9 21.6 %down.4 = bf16[128,2048]{1,0:T(8,128)(2,1)} custom-call(bf16[128,14336]{1,0:T(8,128)(2,1)} %copy.22.h_ref, bf16[14336,2048]{1,0:T(8,128)(2,1)} %expand_out.1.w_ref, bf16[128,2048]{1,0:T(8,128)(2,1)} %x_ref.1), custom_call_target="tpu_custom_call" | custom-call | tf_op jit(solution)/shard_map/down/pallas_call | solution.py:126
  268.5 11.4 %collective-permute-done.x_ref = bf16[128,2048]{1,0:T(8,128)(2,1)S(1)} collective-permute-done((bf16[128,2048]{1,0:T(8,128)(2,1)}, bf16[128,2048]{1,0:T(8,128)(2,1)S(1)}, u32[]{:S(2)}, u32[]{:S(2)}) %collective-permute-start) | collective-permute-done | bytes 524320 | tf_op jit(solution)/shard_map/ppermute | solution.py:167
  281.0 24.6 %all-gather.13.cloned.1.call-done = bf16[128,8192]{1,0:T(8,128)(2,1)} async-done(((bf16[128,2048]{1,0:T(8,128)(2,1)}), bf16[128,8192]{1,0:T(8,128)(2,1)}) %all-gather.13.cloned.1.call-update) | async-done | bytes 2097168 | tf_op jit(solution)/shard_map/all_gather | solution.py:158
  319.3 47.4 %gate_up.5 = bf16[128,3584]{1,0:T(8,128)(2,1)} custom-call(bf16[128,8192]{1,0:T(8,128)(2,1)} %bitcast.67, bf16[8192,7168]{1,0:T(8,128)(2,1)} %expand_in.1.w_ref), custom_call_target="tpu_custom_call" | custom-call | tf_op jit(solution)/shard_map/gate_up/pallas_call | solution.py:103
  366.7 31.6 %all-gather.15.cloned.1.call-done = bf16[128,14336]{1,0:T(8,128)(2,1)} async-done(((bf16[128,3584]{1,0:T(8,128)(2,1)}), bf16[128,14336]{1,0:T(8,128)(2,1)}) %all-gather.15.cloned.1.call-update) | async-done | bytes 3670032 | tf_op jit(solution)/shard_map/all_gather | solution.py:163
  398.3 6.0 copy.25
  404.3 6.2 copy.26
  410.5 5.9 copy.27.h_ref
  416.4 21.6 %down.5 = bf16[128,2048]{1,0:T(8,128)(2,1)} custom-call(bf16[128,14336]{1,0:T(8,128)(2,1)} %copy.27.h_ref, bf16[14336,2048]{1,0:T(8,128)(2,1)} %expand_out.1.w_ref, bf16[128,2048]{1,0:T(8,128)(2,1)} %copy-done.1), custom_call_target="tpu_custom_call" | custom-call | tf_op jit(solution)/shard_map/down/pallas_call | solution.py:126
  441.4 11.9 %collective-permute-done.1.x_ref = bf16[128,2048]{1,0:T(8,128)(2,1)S(1)} collective-permute-done((bf16[128,2048]{1,0:T(8,128)(2,1)}, bf16[128,2048]{1,0:T(8,128)(2,1)S(1)}, u32[]{:S(2)}, u32[]{:S(2)}) %collective-permute-start.1) | collective-permute-done | bytes 524320 | tf_op jit(solution)/shard_map/ppermute | solution.py:167
  454.4 23.4 %all-gather.17.cloned.1.call-done = bf16[128,8192]{1,0:T(8,128)(2,1)} async-done(((bf16[128,2048]{1,0:T(8,128)(2,1)}), bf16[128,8192]{1,0:T(8,128)(2,1)}) %all-gather.17.cloned.1.call-update) | async-done | bytes 2097168 | tf_op jit(solution)/shard_map/all_gather | solution.py:158
  491.5 47.4 %gate_up.6 = bf16[128,3584]{1,0:T(8,128)(2,1)} custom-call(bf16[128,8192]{1,0:T(8,128)(2,1)} %bitcast.68, bf16[8192,7168]{1,0:T(8,128)(2,1)} %expand_in.1.w_ref), custom_call_target="tpu_custom_call" | custom-call | tf_op jit(solution)/shard_map/gate_up/pallas_call | solution.py:103
  538.9 31.6 %all-gather.19.cloned.1.call-done = bf16[128,14336]{1,0:T(8,128)(2,1)} async-done(((bf16[128,3584]{1,0:T(8,128)(2,1)}), bf16[128,14336]{1,0:T(8,128)(2,1)}) %all-gather.19.cloned.1.call-update) | async-done | bytes 3670032 | tf_op jit(solution)/shard_map/all_gather | solution.py:163
  570.5 6.0 copy.30
  576.5 6.2 copy.31
  582.7 5.9 copy.32.h_ref
  588.6 21.6 %down.6 = bf16[128,2048]{1,0:T(8,128)(2,1)} custom-call(bf16[128,14336]{1,0:T(8,128)(2,1)} %copy.32.h_ref, bf16[14336,2048]{1,0:T(8,128)(2,1)} %expand_out.1.w_ref, bf16[128,2048]{1,0:T(8,128)(2,1)} %copy-done.2), custom_call_target="tpu_custom_call" | custom-call | tf_op jit(solution)/shard_map/down/pallas_call | solution.py:126
  613.6 11.9 %collective-permute-done.2.x_ref = bf16[128,2048]{1,0:T(8,128)(2,1)S(1)} collective-permute-done((bf16[128,2048]{1,0:T(8,128)(2,1)}, bf16[128,2048]{1,0:T(8,128)(2,1)S(1)}, u32[]{:S(2)}, u32[]{:S(2)}) %collective-permute-start.2) | collective-permute-done | bytes 524320 | tf_op jit(solution)/shard_map/ppermute | solution.py:167
  626.6 23.3 %all-gather.21.cloned.1.call-done = bf16[128,8192]{1,0:T(8,128)(2,1)} async-done(((bf16[128,2048]{1,0:T(8,128)(2,1)}), bf16[128,8192]{1,0:T(8,128)(2,1)}) %all-gather.21.cloned.1.call-update) | async-done | bytes 2097168 | tf_op jit(solution)/shard_map/all_gather | solution.py:158
  663.7 47.4 %gate_up.7 = bf16[128,3584]{1,0:T(8,128)(2,1)} custom-call(bf16[128,8192]{1,0:T(8,128)(2,1)} %bitcast.65, bf16[8192,7168]{1,0:T(8,128)(2,1)} %expand_in.1.w_ref), custom_call_target="tpu_custom_call" | custom-call | tf_op jit(solution)/shard_map/gate_up/pallas_call | solution.py:103
  711.1 31.7 %all-gather.23.cloned.1.call-done = bf16[128,14336]{1,0:T(8,128)(2,1)} async-done(((bf16[128,3584]{1,0:T(8,128)(2,1)}), bf16[128,14336]{1,0:T(8,128)(2,1)}) %all-gather.23.cloned.1.call-update) | async-done | bytes 3670032 | tf_op jit(solution)/shard_map/all_gather | solution.py:163
  742.7 6.0 copy.35
  748.8 6.3 copy.36
  755.1 6.1 copy.37.h_ref
  761.2 22.0 %down.7 = bf16[128,2048]{1,0:T(8,128)(2,1)} custom-call(bf16[128,14336]{1,0:T(8,128)(2,1)} %copy.37.h_ref, bf16[14336,2048]{1,0:T(8,128)(2,1)} %expand_out.1.w_ref, bf16[128,2048]{1,0:T(8,128)(2,1)} %copy-done), custom_call_target="tpu_custom_call" | custom-call | tf_op jit(solution)/shard_map/down/pallas_call | solution.py:126
  (60 shorter events, 72.3 us)
Async XLA Ops:
  6.5 86.7 %all-gather.9.cloned.1.call-start = ((), (), s32[]{:S(2)}) async-start(), calls=%async_computation | async-start | bytes 2621440 | tf_op jit(solution)/shard_map/all_gather | solution.py:158
  7.3 216.5 %all-gather.11.cloned.1.call-start = ((), (), s32[]{:S(2)}) async-start(), calls=%async_computation.1 | async-start | bytes 4587520 | tf_op jit(solution)/shard_map/all_gather | solution.py:163
  7.3 88.0 %copy-start.6 = (f32[1,8192]{1,0:T(1,128)S(1)}, f32[1,8192]{1,0:T(1,128)}, u32[]{:S(2)}) copy-start(f32[1,8192]{1,0:T(1,128)} %param.8) | copy-start | bytes 98308
  154.3 151.2 %all-gather.13.cloned.1.call-start = ((), (), s32[]{:S(2)}) async-start(), calls=%async_computation.2 | async-start | bytes 2621440 | tf_op jit(solution)/shard_map/all_gather | solution.py:158
  263.5 16.4 %collective-permute-start = (bf16[128,2048]{1,0:T(8,128)(2,1)}, bf16[128,2048]{1,0:T(8,128)(2,1)S(1)}, u32[]{:S(2)}, u32[]{:S(2)}) collective-permute-start(bf16[128,2048]{1,0:T(8,128)(2,1)} %down.4), channel_id=1, source_target_pairs={{0,4},{4,8},{8,12},{1,5},{5,9},{9,13},{2,6},{6,10},{10,14},{3,7},{... | collective-permute-start | bytes 1572872 | tf_op jit(solution)/shard_map/ppermute | solution.py:167
  279.9 0.8 copy-start.1
  280.7 117.6 %all-gather.15.cloned.1.call-start = ((), (), s32[]{:S(2)}) async-start(), calls=%async_computation.3 | async-start | bytes 4587520 | tf_op jit(solution)/shard_map/all_gather | solution.py:163
  366.7 111.1 %all-gather.17.cloned.1.call-start = ((), (), s32[]{:S(2)}) async-start(), calls=%async_computation.4 | async-start | bytes 2621440 | tf_op jit(solution)/shard_map/all_gather | solution.py:158
  438.0 15.3 %collective-permute-start.1 = (bf16[128,2048]{1,0:T(8,128)(2,1)}, bf16[128,2048]{1,0:T(8,128)(2,1)S(1)}, u32[]{:S(2)}, u32[]{:S(2)}) collective-permute-start(bf16[128,2048]{1,0:T(8,128)(2,1)} %down.5), channel_id=1, source_target_pairs={{0,4},{4,8},{8,12},{1,5},{5,9},{9,13},{2,6},{6,10},{10,14},{3,7},{... | collective-permute-start | bytes 1572872 | tf_op jit(solution)/shard_map/ppermute | solution.py:167
  453.3 0.8 copy-start.2
  454.1 116.4 %all-gather.19.cloned.1.call-start = ((), (), s32[]{:S(2)}) async-start(), calls=%async_computation.5 | async-start | bytes 4587520 | tf_op jit(solution)/shard_map/all_gather | solution.py:163
  538.9 111.1 %all-gather.21.cloned.1.call-start = ((), (), s32[]{:S(2)}) async-start(), calls=%async_computation.6 | async-start | bytes 2621440 | tf_op jit(solution)/shard_map/all_gather | solution.py:158
  610.2 15.3 %collective-permute-start.2 = (bf16[128,2048]{1,0:T(8,128)(2,1)}, bf16[128,2048]{1,0:T(8,128)(2,1)S(1)}, u32[]{:S(2)}, u32[]{:S(2)}) collective-permute-start(bf16[128,2048]{1,0:T(8,128)(2,1)} %down.6), channel_id=1, source_target_pairs={{0,4},{4,8},{8,12},{1,5},{5,9},{9,13},{2,6},{6,10},{10,14},{3,7},{... | collective-permute-start | bytes 1572872 | tf_op jit(solution)/shard_map/ppermute | solution.py:167
  625.5 0.8 copy-start
  626.3 116.4 %all-gather.23.cloned.1.call-start = ((), (), s32[]{:S(2)}) async-start(), calls=%async_computation.7 | async-start | bytes 4587520 | tf_op jit(solution)/shard_map/all_gather | solution.py:163
  761.1 22.0 %copy-start.3 = (bf16[128,2048]{1,0:T(8,128)(2,1)S(1)}, bf16[128,2048]{1,0:T(8,128)(2,1)}, u32[]{:S(2)}) copy-start(bf16[128,2048]{1,0:T(8,128)(2,1)} %down.4) | copy-start | bytes 1572868
  761.2 22.0 %copy-start.4 = (bf16[128,2048]{1,0:T(8,128)(2,1)S(1)}, bf16[128,2048]{1,0:T(8,128)(2,1)}, u32[]{:S(2)}) copy-start(bf16[128,2048]{1,0:T(8,128)(2,1)} %down.5) | copy-start | bytes 1572868
  761.2 22.0 %copy-start.5 = (bf16[128,2048]{1,0:T(8,128)(2,1)S(1)}, bf16[128,2048]{1,0:T(8,128)(2,1)}, u32[]{:S(2)}) copy-start(bf16[128,2048]{1,0:T(8,128)(2,1)} %down.6) | copy-start | bytes 1572868
Sparse Core Ops, SparseCore 0:
  8.9 25.2 all-gather.8
  154.4 33.7 all-gather.10
  280.9 24.6 all-gather.12
  366.8 31.4 all-gather.14
  454.2 23.4 all-gather.16
  539.0 31.4 all-gather.18
  626.4 23.4 all-gather.20
  711.2 31.5 all-gather.22

commit v2 on v1

v2 whole, which is shorter than its diff:
```python
import math

import jax
import jax.numpy as jnp
from jax import lax
from jax.experimental import pallas as pl
from jax.experimental.pallas import tpu as pltpu
from jax.sharding import PartitionSpec as P

BS = 64
LANES = 2 * BS
VMEM_LIMIT = 56 * 1024 * 1024


def swap_halves(value):
    return jnp.concatenate([value[:, BS:], value[:, :BS]], axis=1)


def picks_of(index_row, row_blocks):
    slots = index_row.shape[1]
    rows = lax.broadcasted_iota(jnp.int32, (row_blocks, slots), 0)
    return (index_row == rows).astype(jnp.float32).astype(jnp.bfloat16)


def store_rows(even, odd, pair, groups, out_ref):
    base = 0
    for first, count in groups:
        rows = jnp.concatenate([even[first : first + count], odd[first : first + count]], axis=0)
        at = base + 2 * pair * count
        out_ref[at : at + 2 * count, :] = rows.astype(jnp.bfloat16)
        base += BS * count


def expand_in_kernel(row_blocks, groups, index_ref, gate_ref, up_ref, out_ref):
    picks = picks_of(index_ref[0], row_blocks)
    slots = gate_ref.shape[1]
    low = lax.broadcasted_iota(jnp.int32, (slots, LANES), 1) < BS
    for pair in range(BS // 2):
        gate = gate_ref[0, :, pair * LANES : (pair + 1) * LANES]
        up = up_ref[0, :, pair * LANES : (pair + 1) * LANES]
        both = jnp.concatenate(
            [jnp.where(low, gate, swap_halves(up)), jnp.where(low, swap_halves(gate), up)], axis=1
        )
        dense = jnp.dot(picks, both, preferred_element_type=jnp.float32)
        store_rows(dense[:, :LANES], dense[:, LANES:], pair, groups, out_ref)


def cost(flops, *arrays):
    moved = sum(math.prod(a.shape) * a.dtype.itemsize for a in arrays)
    return pl.CostEstimate(flops=flops, bytes_accessed=moved, transcendentals=0)


def expand_in(index, gate_blocks, up_blocks, row_blocks, groups):
    tiles, slots, size = gate_blocks.shape
    padded = tiles + tiles % 2
    shape = jax.ShapeDtypeStruct((row_blocks * BS, padded * LANES), jnp.bfloat16)
    return pl.pallas_call(
        lambda *refs: expand_in_kernel(row_blocks, groups, *refs),
        grid=(tiles,),
        in_specs=[
            pl.BlockSpec((1, 1, slots), lambda c: (c, 0, 0)),
            pl.BlockSpec((1, slots, size), lambda c: (c, 0, 0)),
            pl.BlockSpec((1, slots, size), lambda c: (c, 0, 0)),
        ],
        out_specs=pl.BlockSpec((row_blocks * BS, LANES), lambda c: (0, c)),
        out_shape=shape,
        compiler_params=pltpu.CompilerParams(vmem_limit_bytes=VMEM_LIMIT),
        cost_estimate=cost(0, gate_blocks, up_blocks, shape),
        name="expand_in",
    )(index[:, None, :], gate_blocks, up_blocks)


def expand_out_kernel(row_blocks, chunks, index_ref, blocks_ref, *out_refs):
    first = picks_of(index_ref[0, 0:1, :], row_blocks)
    second = picks_of(index_ref[0, 1:2, :], row_blocks)
    low = lax.broadcasted_iota(jnp.int32, (row_blocks, LANES), 1) < BS
    for quad in range(BS // 4):
        cols = slice(quad * 2 * LANES, (quad + 1) * 2 * LANES)
        left = jnp.dot(first, blocks_ref[0, :, cols], preferred_element_type=jnp.float32)
        right = jnp.dot(second, blocks_ref[1, :, cols], preferred_element_type=jnp.float32)
        for half in range(2):
            a = left[:, half * LANES : (half + 1) * LANES]
            b = right[:, half * LANES : (half + 1) * LANES]
            even = jnp.where(low, a, pltpu.roll(b, BS, 1))
            odd = jnp.where(low, pltpu.roll(a, BS, 1), b)
            for groups, out_ref in zip(chunks, out_refs):
                store_rows(even, odd, 2 * quad + half, groups, out_ref)


def expand_out(index, blocks, row_blocks, chunks):
    tiles, slots, size = blocks.shape
    depths = [BS * sum(count for _, count in groups) for groups in chunks]
    shapes = [jax.ShapeDtypeStruct((depth, tiles * BS), jnp.bfloat16) for depth in depths]
    return pl.pallas_call(
        lambda *refs: expand_out_kernel(row_blocks, chunks, *refs),
        grid=(tiles // 2,),
        in_specs=[
            pl.BlockSpec((1, 2, slots), lambda c: (c, 0, 0)),
            pl.BlockSpec((2, slots, size), lambda c: (c, 0, 0)),
        ],
        out_specs=[pl.BlockSpec((depth, LANES), lambda c: (0, c)) for depth in depths],
        out_shape=shapes,
        compiler_params=pltpu.CompilerParams(vmem_limit_bytes=VMEM_LIMIT),
        cost_estimate=cost(0, blocks, *shapes),
        name="expand_out",
    )(index.reshape(tiles // 2, 2, slots), blocks)


def gate_up_kernel(x_ref, w_ref, out_ref):
    both = jnp.dot(x_ref[...], w_ref[...], preferred_element_type=jnp.float32)
    a, b = both[:, :LANES], both[:, LANES:]
    low = lax.broadcasted_iota(jnp.int32, a.shape, 1) < BS
    gate = jnp.where(low, a, pltpu.roll(b, BS, 1))
    up = jnp.where(low, pltpu.roll(a, BS, 1), b)
    out_ref[...] = (gate / (1.0 + jnp.exp(-gate)) * up).astype(jnp.bfloat16)


def gate_up(x, weights, first, steps):
    rows, depth = x.shape
    shape = jax.ShapeDtypeStruct((rows, steps * LANES), jnp.bfloat16)
    used = jax.ShapeDtypeStruct((depth, steps * 2 * LANES), jnp.bfloat16)
    return pl.pallas_call(
        gate_up_kernel,
        grid=(steps,),
        in_specs=[
            pl.BlockSpec((rows, depth), lambda n: (0, 0)),
            pl.BlockSpec((depth, 2 * LANES), lambda n: (0, n + first)),
        ],
        out_specs=pl.BlockSpec((rows, LANES), lambda n: (0, n)),
        out_shape=shape,
        compiler_params=pltpu.CompilerParams(vmem_limit_bytes=VMEM_LIMIT),
        cost_estimate=cost(2 * rows * depth * steps * 2 * LANES, x, used, shape),
        name="gate_up",
    )(x, weights)


def down_kernel(h_ref, w_ref, total_ref, out_ref):
    mixed = jnp.dot(h_ref[...], w_ref[...], preferred_element_type=jnp.float32)
    out_ref[...] = (total_ref[...].astype(jnp.float32) + mixed).astype(out_ref.dtype)


def down(hidden, weights, total, dtype):
    rows, depth = hidden.shape
    cols = weights.shape[1]
    width = 2 * LANES if cols % (2 * LANES) == 0 else LANES
    shape = jax.ShapeDtypeStruct((rows, cols), dtype)
    return pl.pallas_call(
        down_kernel,
        grid=(cols // width,),
        in_specs=[
            pl.BlockSpec((rows, depth), lambda n: (0, 0)),
            pl.BlockSpec((depth, width), lambda n: (0, n)),
            pl.BlockSpec((rows, width), lambda n: (0, n)),
        ],
        out_specs=pl.BlockSpec((rows, width), lambda n: (0, n)),
        out_shape=shape,
        compiler_params=pltpu.CompilerParams(vmem_limit_bytes=VMEM_LIMIT),
        cost_estimate=cost(2 * rows * depth * cols, hidden, weights, total, shape),
        name="down",
    )(hidden, weights, total)


def by_inner_row(value, groups=1):
    rows, cols = value.shape
    split = value.reshape(rows, groups, cols // (groups * BS), BS)
    return split.swapaxes(2, 3).reshape(rows, cols)


def gathered(value, split):
    if split:
        return lax.all_gather(by_inner_row(value), "tensor", axis=1, tiled=True)
    return by_inner_row(lax.all_gather(value, "tensor", axis=1, tiled=True))


def local(x_in, norm_gain, in_index, gate_blocks, up_blocks, out_index, down_blocks):
    segment_count = lax.axis_size("segment")
    devices = lax.axis_size("tensor")
    segment_at = lax.axis_index("segment")
    gain_row = norm_gain[0]
    tiles = in_index.shape[1]
    in_blocks = gain_row.shape[0] // BS
    per_device = in_blocks // devices
    split_in = per_device % 8 == 0
    groups_in = [(d * per_device, per_device) for d in range(devices)] if split_in else [(0, in_blocks)]
    gain_row = by_inner_row(gain_row[None, :], len(groups_in))
    split_out = tiles % 8 == 0
    if split_out:
        early = -(-tiles // 16) * 8
        parts = [(0, early), (early, tiles - early)] if early < tiles else [(0, tiles)]
        chunks = [[(d * tiles + at, count) for d in range(devices)] for at, count in parts]
    else:
        parts = [(0, tiles)]
        chunks = [[(0, devices * tiles)]]
    weights_in = expand_in(in_index[0], gate_blocks[0], up_blocks[0], in_blocks, groups_in)
    weights_out = expand_out(out_index[0], down_blocks[0], devices * tiles, chunks)
    pairs = [(i, i + 1) for i in range(segment_count - 1)]
    incoming = x_in
    result = jnp.zeros_like(x_in)
    for tick in range(segment_count):
        wide = gathered(incoming, split_in).astype(jnp.float32)
        stat = jnp.mean(wide * wide, axis=1, keepdims=True)
        normed = (wide * lax.rsqrt(stat + 1e-05) * gain_row).astype(jnp.bfloat16)
        hidden = []
        for at, count in parts:
            part = gate_up(normed, weights_in, at // 2, -(-count // 2))[:, : count * BS]
            hidden.append(gathered(part, split_out))
        total = incoming
        for order, (part, weights) in enumerate(zip(hidden, weights_out)):
            last = order + 1 == len(hidden)
            total = down(part, weights, total, jnp.bfloat16 if last else jnp.float32)
        result = jnp.where(segment_at == tick, total, result)
        if tick + 1 < segment_count:
            incoming = lax.ppermute(total, "segment", pairs)
    return result[None]


def solution(mesh):
    placed = (
        P("replica", "tensor"),
        P("segment", None),
        P("segment", "tensor", None),
        P("segment", "tensor", None, None),
        P("segment", "tensor", None, None),
        P("segment", "tensor", None),
        P("segment", "tensor", None, None),
    )
    return jax.shard_map(
        local,
        mesh=mesh,
        in_specs=placed,
        out_specs=P("segment", "replica", "tensor"),
        check_vma=False,
    )
```

time: 802 us -> 674 us (0.84)
  local copies, waits for them, and re-layouts: 144 us -> 59.5 us
  waiting for transfers between devices: 202 us -> 120 us
  Pallas kernels: 400 us -> 438 us
    all_gather x8 -> x12, waiting for transfers between devices: 166 us -> 85 us  [gathered(): return lax.all_gather(by_inner_row(value), 'tensor', axis=1, tiled=True)]
    transpose x8 -> x12, local copies, waits for them, and re-layouts: 40.2 us -> 3.79 us  [by_inner_row(): return split.swapaxes(2, 3).reshape(rows, cols)]
    pallas_call x4 -> x8, Pallas kernels: 86.7 us -> 113 us  [down(): pl.pallas_call(down_kernel, grid=(cols // width,), in_specs=[pl.BlockSpec...]
    all_gather x4 -> x0, local copies, waits for them, and re-layouts: 24 us -> none  [local(): hidden = lax.all_gather(hidden, 'tensor', axis=1, tiled=True)]
    unnamed x19 -> x15, local copies, waits for them, and re-layouts: 45.7 us -> 32.5 us
    reshape x4 -> x12, local copies, waits for them, and re-layouts: 23.9 us -> 12 us  [by_inner_row(): return split.swapaxes(2, 3).reshape(rows, cols)]
    pallas_call x4 -> x8, Pallas kernels: 189 us -> 201 us  [gate_up(): pl.pallas_call(gate_up_kernel, grid=(steps,), in_specs=[pl.BlockSpec((row...]
    pallas_call x0 -> x8, local copies, waits for them, and re-layouts: none -> 10.1 us  [gate_up(): pl.pallas_call(gate_up_kernel, grid=(steps,), in_specs=[pl.BlockSpec((row...]
  transfers between devices with their start and end apart: 11 -> 15, of which waited for: 9 -> 9; matrix products, arithmetic and copies ran while one was open for 4% -> 6% of each run, Pallas kernels for 16% -> 41%
where the time goes in v2:
time: 674 us; the launch traced here: 669 us
  Pallas kernels  438 us (65%)
  waiting for transfers between devices  120 us (18%)
  local copies, waits for them, and re-layouts  59.5 us (9%)
  other arithmetic  24.7 us (4%)
  between operations  13.9 us (2%)
  starting transfers between devices  12.7 us (2%)
    pallas_call x8, Pallas kernels, gate_up(): pl.pallas_call(gate_up_kernel, grid=(steps,), in_specs=[pl.BlockSpec((row...  201 us
    pallas_call x8, Pallas kernels, down(): pl.pallas_call(down_kernel, grid=(cols // width,), in_specs=[pl.BlockSpec...  113 us
    pallas_call x1, Pallas kernels, expand_in(): pl.pallas_call(lambda *refs: expand_in_kernel(row_blocks, groups, *refs),...  85.9 us
    all_gather x12, waiting for transfers between devices, gathered(): return lax.all_gather(by_inner_row(value), 'tensor', axis=1, tiled=True)  85 us
    pallas_call x1, Pallas kernels, expand_out(): pl.pallas_call(lambda *refs: expand_out_kernel(row_blocks, chunks, *refs)...  38.1 us
    ppermute x3, waiting for transfers between devices, local(): incoming = lax.ppermute(total, 'segment', pairs)  34.9 us
    unnamed x15, local copies, waits for them, and re-layouts  32.5 us
    convert_element_type x4, other arithmetic, local(): normed = (wide * lax.rsqrt(stat + 1e-05) * gain_row).astype(jnp.bfloat16)  13.9 us
  transfers between devices with their start and end apart: 15, of which 9 were waited for; matrix products, arithmetic and copies ran while one was open for 6% of the time, Pallas kernels for 41%

profile of v2, /device:TPU:0, one launch (start us, length us, event | category | flops | bytes accessed | tf_op | source)
XLA Modules:
  0.0 668.6 jit_solution(14202808541919541059)
XLA Ops:
  11.7 85.9 %expand_in.1.w_ref = bf16[8192,7168]{1,0:T(8,128)(2,1)} custom-call(s32[56,1,72]{2,1,0:T(1,128)} %bitcast.88, bf16[56,72,4096]{2,1,0:T(8,128)(2,1)} %bitcast.61, bf16[56,72,4096]{2,1,0:T(8,128)(2,1)} %bitcast.62), custom_call_target="tpu_custom_call" | custom-call | bytes 183500800 | tf_op jit(solution)/shard_map/expand_in/pallas_call | solution.py:57
  99.7 3.5 fusion.2.x_ref
  103.2 28.1 %gate_up.9 = bf16[128,2048]{1,0:T(8,128)(2,1)} custom-call(bf16[128,8192]{1,0:T(8,128)(2,1)} %fusion.2.x_ref, bf16[8192,7168]{1,0:T(8,128)(2,1)} %expand_in.1.w_ref), custom_call_target="tpu_custom_call" | custom-call | flops 8589934592 | bytes 69730304 | tf_op jit(solution)/shard_map/gate_up/pallas_call | solution.py:122
  134.0 22.1 %gate_up.8 = bf16[128,1536]{1,0:T(8,128)(2,1)} custom-call(bf16[128,8192]{1,0:T(8,128)(2,1)} %fusion.2.x_ref, bf16[8192,7168]{1,0:T(8,128)(2,1)} %expand_in.1.w_ref), custom_call_target="tpu_custom_call" | custom-call | flops 6442450944 | bytes 52822016 | tf_op jit(solution)/shard_map/gate_up/pallas_call | solution.py:122
  158.7 30.6 %copy.60 = bf16[1,32,126,4096]{3,2,1,0:T(8,128)(2,1)} copy(bf16[1,32,126,4096]{3,1,2,0:T(8,128)(2,1)} %param.13) | data formatting | bytes 66060288 | tf_op args[6]
  189.3 38.1 %expand_out.1 = (bf16[8192,2048]{1,0:T(8,128)(2,1)}, bf16[6144,2048]{1,0:T(8,128)(2,1)}) custom-call(s32[16,2,126]{2,1,0:T(2,128)} %bitcast.89, bf16[32,126,4096]{2,1,0:T(8,128)(2,1)} %bitcast.60), custom_call_target="tpu_custom_call" | custom-call | bytes 91750400 | tf_op jit(solution)/shard_map/expand_out/pallas_call | solution.py:94
  227.4 15.2 %down.8.total_ref = f32[128,2048]{1,0:T(8,128)} custom-call(bf16[128,8192]{1,0:T(8,128)(2,1)} %all-gather.17.cloned.1.call-done.h_ref, bf16[8192,2048]{1,0:T(8,128)(2,1)} %get-tuple-element.8.w_ref, bf16[128,2048]{1,0:T(8,128)(2,1)} %total_ref.1), custom_call_target="tpu_custom_call" | custom-call | flops 4294967296 | bytes 37224448 | tf_op jit(solution)/shard_map/down/pallas_call | solution.py:147
  242.6 12.8 %down.9 = bf16[128,2048]{1,0:T(8,128)(2,1)} custom-call(bf16[128,6144]{1,0:T(8,128)(2,1)} %all-gather.15.cloned.1.call-done.h_ref, bf16[6144,2048]{1,0:T(8,128)(2,1)} %get-tuple-element.7.w_ref, f32[128,2048]{1,0:T(8,128)} %down.8.total_ref), custom_call_target="tpu_custom_call" | custom-call | flops 3221225472 | bytes 28311552 | tf_op jit(solution)/shard_map/down/pallas_call | solution.py:147
  255.4 5.0 collective-permute-start
  260.5 11.5 %collective-permute-done.total_ref = bf16[128,2048]{1,0:T(8,128)(2,1)S(1)} collective-permute-done((bf16[128,2048]{1,0:T(8,128)(2,1)}, bf16[128,2048]{1,0:T(8,128)(2,1)S(1)}, u32[]{:S(2)}, u32[]{:S(2)}) %collective-permute-start) | collective-permute-done | bytes 524320 | tf_op jit(solution)/shard_map/ppermute | solution.py:213
  273.9 24.6 %all-gather.19.cloned.1.call-done = bf16[128,8192]{1,0:T(8,128)(2,1)} async-done(((bf16[128,2048]{1,0:T(8,128)(2,1)}), bf16[128,8192]{1,0:T(8,128)(2,1)}) %all-gather.19.cloned.1.call-update) | async-done | bytes 2097168 | tf_op jit(solution)/shard_map/all_gather | solution.py:171
  300.6 3.5 fusion.5.x_ref
  304.0 28.1 %gate_up.11 = bf16[128,2048]{1,0:T(8,128)(2,1)} custom-call(bf16[128,8192]{1,0:T(8,128)(2,1)} %fusion.5.x_ref, bf16[8192,7168]{1,0:T(8,128)(2,1)} %expand_in.1.w_ref), custom_call_target="tpu_custom_call" | custom-call | flops 8589934592 | bytes 69730304 | tf_op jit(solution)/shard_map/gate_up/pallas_call | solution.py:122
  334.9 22.1 %gate_up.10 = bf16[128,1536]{1,0:T(8,128)(2,1)} custom-call(bf16[128,8192]{1,0:T(8,128)(2,1)} %fusion.5.x_ref, bf16[8192,7168]{1,0:T(8,128)(2,1)} %expand_in.1.w_ref), custom_call_target="tpu_custom_call" | custom-call | flops 6442450944 | bytes 52822016 | tf_op jit(solution)/shard_map/gate_up/pallas_call | solution.py:122
  359.5 15.5 %down.10.total_ref = f32[128,2048]{1,0:T(8,128)} custom-call(bf16[128,8192]{1,0:T(8,128)(2,1)} %all-gather.23.cloned.1.call-done.h_ref, bf16[8192,2048]{1,0:T(8,128)(2,1)} %get-tuple-element.8.w_ref, bf16[128,2048]{1,0:T(8,128)(2,1)} %copy-done.1), custom_call_target="tpu_custom_call" | custom-call | flops 4294967296 | bytes 37224448 | tf_op jit(solution)/shard_map/down/pallas_call | solution.py:147
  375.0 4.4 all-gather.21.cloned.1.call-done.h_ref
  379.4 12.8 %down.11 = bf16[128,2048]{1,0:T(8,128)(2,1)} custom-call(bf16[128,6144]{1,0:T(8,128)(2,1)} %all-gather.21.cloned.1.call-done.h_ref, bf16[6144,2048]{1,0:T(8,128)(2,1)} %get-tuple-element.7.w_ref, f32[128,2048]{1,0:T(8,128)} %down.10.total_ref), custom_call_target="tpu_custom_call" | custom-call | flops 3221225472 | bytes 28311552 | tf_op jit(solution)/shard_map/down/pallas_call | solution.py:147
  395.6 11.8 %collective-permute-done.1.total_ref = bf16[128,2048]{1,0:T(8,128)(2,1)S(1)} collective-permute-done((bf16[128,2048]{1,0:T(8,128)(2,1)}, bf16[128,2048]{1,0:T(8,128)(2,1)S(1)}, u32[]{:S(2)}, u32[]{:S(2)}) %collective-permute-start.1) | collective-permute-done | bytes 524320 | tf_op jit(solution)/shard_map/ppermute | solution.py:213
  409.2 23.6 %all-gather.25.cloned.1.call-done = bf16[128,8192]{1,0:T(8,128)(2,1)} async-done(((bf16[128,2048]{1,0:T(8,128)(2,1)}), bf16[128,8192]{1,0:T(8,128)(2,1)}) %all-gather.25.cloned.1.call-update) | async-done | bytes 2097168 | tf_op jit(solution)/shard_map/all_gather | solution.py:171
  438.3 28.1 %gate_up.13 = bf16[128,2048]{1,0:T(8,128)(2,1)} custom-call(bf16[128,8192]{1,0:T(8,128)(2,1)} %fusion.8.x_ref, bf16[8192,7168]{1,0:T(8,128)(2,1)} %expand_in.1.w_ref), custom_call_target="tpu_custom_call" | custom-call | flops 8589934592 | bytes 69730304 | tf_op jit(solution)/shard_map/gate_up/pallas_call | solution.py:122
  469.2 22.1 %gate_up.12 = bf16[128,1536]{1,0:T(8,128)(2,1)} custom-call(bf16[128,8192]{1,0:T(8,128)(2,1)} %fusion.8.x_ref, bf16[8192,7168]{1,0:T(8,128)(2,1)} %expand_in.1.w_ref), custom_call_target="tpu_custom_call" | custom-call | flops 6442450944 | bytes 52822016 | tf_op jit(solution)/shard_map/gate_up/pallas_call | solution.py:122
  493.9 15.5 %down.12.total_ref = f32[128,2048]{1,0:T(8,128)} custom-call(bf16[128,8192]{1,0:T(8,128)(2,1)} %all-gather.29.cloned.1.call-done.h_ref, bf16[8192,2048]{1,0:T(8,128)(2,1)} %get-tuple-element.8.w_ref, bf16[128,2048]{1,0:T(8,128)(2,1)} %copy-done.2), custom_call_target="tpu_custom_call" | custom-call | flops 4294967296 | bytes 37224448 | tf_op jit(solution)/shard_map/down/pallas_call | solution.py:147
  509.3 4.4 all-gather.27.cloned.1.call-done.h_ref
  513.7 12.8 %down.13 = bf16[128,2048]{1,0:T(8,128)(2,1)} custom-call(bf16[128,6144]{1,0:T(8,128)(2,1)} %all-gather.27.cloned.1.call-done.h_ref, bf16[6144,2048]{1,0:T(8,128)(2,1)} %get-tuple-element.7.w_ref, f32[128,2048]{1,0:T(8,128)} %down.12.total_ref), custom_call_target="tpu_custom_call" | custom-call | flops 3221225472 | bytes 28311552 | tf_op jit(solution)/shard_map/down/pallas_call | solution.py:147
  526.5 3.6 collective-permute-start.2
  530.2 11.6 %collective-permute-done.2.total_ref = bf16[128,2048]{1,0:T(8,128)(2,1)S(1)} collective-permute-done((bf16[128,2048]{1,0:T(8,128)(2,1)}, bf16[128,2048]{1,0:T(8,128)(2,1)S(1)}, u32[]{:S(2)}, u32[]{:S(2)}) %collective-permute-start.2) | collective-permute-done | bytes 524320 | tf_op jit(solution)/shard_map/ppermute | solution.py:213
  543.5 23.6 %all-gather.31.cloned.1.call-done = bf16[128,8192]{1,0:T(8,128)(2,1)} async-done(((bf16[128,2048]{1,0:T(8,128)(2,1)}), bf16[128,8192]{1,0:T(8,128)(2,1)}) %all-gather.31.cloned.1.call-update) | async-done | bytes 2097168 | tf_op jit(solution)/shard_map/all_gather | solution.py:171
  572.7 28.1 %gate_up.15 = bf16[128,2048]{1,0:T(8,128)(2,1)} custom-call(bf16[128,8192]{1,0:T(8,128)(2,1)} %fusion.11.x_ref, bf16[8192,7168]{1,0:T(8,128)(2,1)} %expand_in.1.w_ref), custom_call_target="tpu_custom_call" | custom-call | flops 8589934592 | bytes 69730304 | tf_op jit(solution)/shard_map/gate_up/pallas_call | solution.py:122
  603.6 22.1 %gate_up.14 = bf16[128,1536]{1,0:T(8,128)(2,1)} custom-call(bf16[128,8192]{1,0:T(8,128)(2,1)} %fusion.11.x_ref, bf16[8192,7168]{1,0:T(8,128)(2,1)} %expand_in.1.w_ref), custom_call_target="tpu_custom_call" | custom-call | flops 6442450944 | bytes 52822016 | tf_op jit(solution)/shard_map/gate_up/pallas_call | solution.py:122
  628.1 15.5 %down.14.total_ref = f32[128,2048]{1,0:T(8,128)} custom-call(bf16[128,8192]{1,0:T(8,128)(2,1)} %all-gather.35.cloned.1.call-done.h_ref, bf16[8192,2048]{1,0:T(8,128)(2,1)} %get-tuple-element.8.w_ref, bf16[128,2048]{1,0:T(8,128)(2,1)} %copy-done), custom_call_target="tpu_custom_call" | custom-call | flops 4294967296 | bytes 37224448 | tf_op jit(solution)/shard_map/down/pallas_call | solution.py:147
  643.6 4.4 all-gather.33.cloned.1.call-done.h_ref
  648.0 12.8 %down.15 = bf16[128,2048]{1,0:T(8,128)(2,1)} custom-call(bf16[128,6144]{1,0:T(8,128)(2,1)} %all-gather.33.cloned.1.call-done.h_ref, bf16[6144,2048]{1,0:T(8,128)(2,1)} %get-tuple-element.7.w_ref, f32[128,2048]{1,0:T(8,128)} %down.14.total_ref), custom_call_target="tpu_custom_call" | custom-call | flops 3221225472 | bytes 28311552 | tf_op jit(solution)/shard_map/down/pallas_call | solution.py:147
  (95 shorter events, 50.9 us)
Async XLA Ops:
  6.5 91.1 %all-gather.13.cloned.1.call-start = ((), (), s32[]{:S(2)}) async-start(), calls=%async_computation | async-start | bytes 2621440 | tf_op jit(solution)/shard_map/all_gather | solution.py:171
  9.2 218.2 %all-gather.17.cloned.1.call-start = ((), (), s32[]{:S(2)}) async-start(), calls=%async_computation.2 | async-start | bytes 2621440 | tf_op jit(solution)/shard_map/all_gather | solution.py:171
  134.0 108.6 %all-gather.15.cloned.1.call-start = ((), (), s32[]{:S(2)}) async-start(), calls=%async_computation.1 | async-start | bytes 1966080 | tf_op jit(solution)/shard_map/all_gather | solution.py:171
  158.6 139.8 %all-gather.19.cloned.1.call-start = ((), (), s32[]{:S(2)}) async-start(), calls=%async_computation.3 | async-start | bytes 2621440 | tf_op jit(solution)/shard_map/all_gather | solution.py:171
  255.4 16.5 %collective-permute-start = (bf16[128,2048]{1,0:T(8,128)(2,1)}, bf16[128,2048]{1,0:T(8,128)(2,1)S(1)}, u32[]{:S(2)}, u32[]{:S(2)}) collective-permute-start(bf16[128,2048]{1,0:T(8,128)(2,1)} %down.9), channel_id=1, source_target_pairs={{0,4},{4,8},{8,12},{1,5},{5,9},{9,13},{2,6},{6,10},{10,14},{3,7},{... | collective-permute-start | bytes 1572872 | tf_op jit(solution)/shard_map/ppermute | solution.py:213
  272.0 32.1 %copy-start.1 = (bf16[128,2048]{1,0:T(8,128)(2,1)}, bf16[128,2048]{1,0:T(8,128)(2,1)S(1)}, u32[]{:S(2)}) copy-start(bf16[128,2048]{1,0:T(8,128)(2,1)S(1)} %collective-permute-done.total_ref) | copy-start | bytes 1572868
  273.7 85.9 %all-gather.23.cloned.1.call-start = ((), (), s32[]{:S(2)}) async-start(), calls=%async_computation.5 | async-start | bytes 2621440 | tf_op jit(solution)/shard_map/all_gather | solution.py:171
  334.9 44.5 %all-gather.21.cloned.1.call-start = ((), (), s32[]{:S(2)}) async-start(), calls=%async_computation.4 | async-start | bytes 1966080 | tf_op jit(solution)/shard_map/all_gather | solution.py:171
  359.4 73.3 %all-gather.25.cloned.1.call-start = ((), (), s32[]{:S(2)}) async-start(), calls=%async_computation.6 | async-start | bytes 2621440 | tf_op jit(solution)/shard_map/all_gather | solution.py:171
  392.2 15.3 %collective-permute-start.1 = (bf16[128,2048]{1,0:T(8,128)(2,1)}, bf16[128,2048]{1,0:T(8,128)(2,1)S(1)}, u32[]{:S(2)}, u32[]{:S(2)}) collective-permute-start(bf16[128,2048]{1,0:T(8,128)(2,1)} %down.11), channel_id=1, source_target_pairs={{0,4},{4,8},{8,12},{1,5},{5,9},{9,13},{2,6},{6,10},{10,14},{3,7},{... | collective-permute-start | bytes 1572872 | tf_op jit(solution)/shard_map/ppermute | solution.py:213
  407.4 30.9 %copy-start.2 = (bf16[128,2048]{1,0:T(8,128)(2,1)}, bf16[128,2048]{1,0:T(8,128)(2,1)S(1)}, u32[]{:S(2)}) copy-start(bf16[128,2048]{1,0:T(8,128)(2,1)S(1)} %collective-permute-done.1.total_ref) | copy-start | bytes 1572868
  409.1 84.7 %all-gather.29.cloned.1.call-start = ((), (), s32[]{:S(2)}) async-start(), calls=%async_computation.8 | async-start | bytes 2621440 | tf_op jit(solution)/shard_map/all_gather | solution.py:171
  469.2 44.5 %all-gather.27.cloned.1.call-start = ((), (), s32[]{:S(2)}) async-start(), calls=%async_computation.7 | async-start | bytes 1966080 | tf_op jit(solution)/shard_map/all_gather | solution.py:171
  493.8 73.3 %all-gather.31.cloned.1.call-start = ((), (), s32[]{:S(2)}) async-start(), calls=%async_computation.9 | async-start | bytes 2621440 | tf_op jit(solution)/shard_map/all_gather | solution.py:171
  526.5 15.3 %collective-permute-start.2 = (bf16[128,2048]{1,0:T(8,128)(2,1)}, bf16[128,2048]{1,0:T(8,128)(2,1)S(1)}, u32[]{:S(2)}, u32[]{:S(2)}) collective-permute-start(bf16[128,2048]{1,0:T(8,128)(2,1)} %down.13), channel_id=1, source_target_pairs={{0,4},{4,8},{8,12},{1,5},{5,9},{9,13},{2,6},{6,10},{10,14},{3,7},{... | collective-permute-start | bytes 1572872 | tf_op jit(solution)/shard_map/ppermute | solution.py:213
  541.8 30.9 %copy-start = (bf16[128,2048]{1,0:T(8,128)(2,1)}, bf16[128,2048]{1,0:T(8,128)(2,1)S(1)}, u32[]{:S(2)}) copy-start(bf16[128,2048]{1,0:T(8,128)(2,1)S(1)} %collective-permute-done.2.total_ref) | copy-start | bytes 1572868
  543.5 84.7 %all-gather.35.cloned.1.call-start = ((), (), s32[]{:S(2)}) async-start(), calls=%async_computation.11 | async-start | bytes 2621440 | tf_op jit(solution)/shard_map/all_gather | solution.py:171
  603.5 44.5 %all-gather.33.cloned.1.call-start = ((), (), s32[]{:S(2)}) async-start(), calls=%async_computation.10 | async-start | bytes 1966080 | tf_op jit(solution)/shard_map/all_gather | solution.py:171
  643.6 17.2 %copy-start.3 = (bf16[128,2048]{1,0:T(8,128)(2,1)S(1)}, bf16[128,2048]{1,0:T(8,128)(2,1)}, u32[]{:S(2)}) copy-start(bf16[128,2048]{1,0:T(8,128)(2,1)} %down.9) | copy-start | bytes 1572868
  643.6 17.2 %copy-start.4 = (bf16[128,2048]{1,0:T(8,128)(2,1)S(1)}, bf16[128,2048]{1,0:T(8,128)(2,1)}, u32[]{:S(2)}) copy-start(bf16[128,2048]{1,0:T(8,128)(2,1)} %down.11) | copy-start | bytes 1572868
  643.6 17.2 %copy-start.5 = (bf16[128,2048]{1,0:T(8,128)(2,1)S(1)}, bf16[128,2048]{1,0:T(8,128)(2,1)}, u32[]{:S(2)}) copy-start(bf16[128,2048]{1,0:T(8,128)(2,1)} %down.13) | copy-start | bytes 1572868
Sparse Core Ops, SparseCore 0:
  9.4 25.2 all-gather.12
  134.1 25.2 all-gather.16
  161.0 20.1 all-gather.14
  273.8 24.6 all-gather.18
  335.0 22.6 all-gather.22
  359.6 19.7 all-gather.20
  409.2 23.4 all-gather.24
  469.3 22.6 all-gather.28
  493.9 19.7 all-gather.26
  543.6 23.4 all-gather.30
  603.7 22.6 all-gather.34
  628.2 19.7 all-gather.32
